TPU v7x, 256 devices: a whole 4x4x8 slice. The times are simulated.
256 devices in a mesh: layer: 4 (over y_lo, core), train: 8 (over y_hi, x), query: 8 (over z).
Axes of the slice: x: 4, y: 4 (y_hi: 2, y_lo: 2; y = y_hi * 2 + y_lo), z: 8, core: 2. Of those that a mesh axis runs over, the one named last changes fastest.
Arguments:
- train_act: bfloat16 [2, 4, 64, 128, 4096], P(None, 'layer', ('train', 'query')), may hold values from -6 to 6
- train_grad: bfloat16 [2, 4, 64, 128, 4096], P(None, 'layer', ('train', 'query')), may hold values from -6 to 6
- query_act: bfloat16 [2, 4, 64, 128, 4096], P(None, 'layer', ('train', 'query')), may hold values from -6 to 6
- query_grad: bfloat16 [2, 4, 64, 128, 4096], P(None, 'layer', ('train', 'query')), may hold values from -6 to 6
- in_projection: bfloat16 [4, 4096, 128], P('layer'), may hold values from -0.09375 to 0.09375
- out_projection: bfloat16 [4, 4096, 64], P('layer'), may hold values from -0.09375 to 0.09375
- inverse_hessian: bfloat16 [2, 8192, 8192], P(None, 'layer', ('train', 'query'))
- train_lengths: int32 [64], P(('train', 'query')), may hold values from 16 to 128
- query_lengths: int32 [64], P(('train', 'query')), may hold values from 16 to 128
Outputs:
- scores: float32 [64, 64], P('train', 'query')
All inputs are finite; a program needn't handle non-finite values.
Results may differ from a plain program's by a relative error of at most 0.0071.
Values may be sent and summed in bfloat16 or wider, within the bound.
No kernel may reach another device: no remote copies, remote signals or barrier semaphores. Data moves between devices by JAX's collectives and lax.ppermute only.
A program may use at most 64 MiB of HBM per device.

v0:
```python
import jax
import jax.numpy as jnp
from jax import lax
from jax.sharding import PartitionSpec as P


def project_rows(activations, gradients, in_projection, out_projection, lengths):
    ckpt_count, layer_count, row_count, seq_len, width = activations.shape
    inner_width = in_projection.shape[2]
    outer_width = out_projection.shape[2]
    positions = lax.broadcasted_iota(jnp.int32, (row_count, seq_len), 1)
    keep_mask = (positions < lengths[:, None]).reshape(1, row_count * seq_len, 1)
    flat_act = activations[:, 0].reshape(ckpt_count, row_count * seq_len, width)
    flat_grad = gradients[:, 0].reshape(ckpt_count, row_count * seq_len, width)
    inner = jnp.einsum(
        "cnd,dk->cnk", flat_act, in_projection[0], preferred_element_type=jnp.float32
    ).astype(jnp.bfloat16)
    outer = jnp.einsum(
        "cnd,dk->cnk", flat_grad, out_projection[0], preferred_element_type=jnp.float32
    )
    outer = jnp.where(keep_mask, outer, 0.0).astype(jnp.bfloat16)
    total = jnp.einsum(
        "cnso,cnsi->cnoi",
        outer.reshape(ckpt_count, row_count, seq_len, outer_width),
        inner.reshape(ckpt_count, row_count, seq_len, inner_width),
        preferred_element_type=jnp.float32,
    )
    return total.reshape(ckpt_count, row_count, outer_width * inner_width)


def score_block(pre_rows, query_columns):
    return jnp.einsum(
        "crk,cqk->rq",
        pre_rows,
        query_columns.astype(jnp.float32),
        precision=lax.Precision.HIGHEST,
        preferred_element_type=jnp.float32,
    )


def on_device(
    train_act,
    train_grad,
    query_act,
    query_grad,
    in_projection,
    out_projection,
    inverse_hessian,
    train_lengths,
    query_lengths,
):
    seq_len = train_act.shape[3]
    train_terms = project_rows(train_act, train_grad, in_projection, out_projection, train_lengths)
    query_terms = project_rows(query_act, query_grad, in_projection, out_projection, query_lengths)
    train_total, query_total = lax.psum((train_terms, query_terms), "layer")
    train_full = (train_total / seq_len).astype(jnp.bfloat16)
    query_full = (query_total / seq_len).astype(jnp.bfloat16)
    block_width = inverse_hessian.shape[1]
    column_width = inverse_hessian.shape[2]
    layer_index = lax.axis_index("layer")
    train_block = lax.dynamic_slice_in_dim(train_full, layer_index * block_width, block_width, 2)
    train_count = lax.axis_size("train")
    query_count = lax.axis_size("query")
    grid_index = lax.axis_index("train") * query_count + lax.axis_index("query")
    train_rows, query_rows = (
        lax.all_gather(train_block, ("train", "query"), axis=1, tiled=True),
        lax.all_gather(query_full, ("train", "query"), axis=1, tiled=True),
    )
    query_columns = lax.dynamic_slice_in_dim(query_rows, grid_index * column_width, column_width, 2)
    partial_pre = jnp.einsum(
        "crk,ckn->crn", train_rows, inverse_hessian, preferred_element_type=jnp.float32
    )
    preconditioned = lax.psum(partial_pre, "layer")
    score_terms = score_block(preconditioned, query_columns)
    total_rows, total_cols = score_terms.shape
    tile_rows = total_rows // train_count
    tile_cols = total_cols // query_count
    arranged = score_terms.reshape(train_count, tile_rows, query_count, tile_cols)
    arranged = jnp.transpose(arranged, (0, 2, 1, 3)).reshape(
        train_count * query_count * tile_rows, tile_cols
    )
    tile = lax.psum_scatter(arranged, ("train", "query"), scatter_dimension=0, tiled=True)
    return tile


def solution(mesh):
    in_specs = (
        P(None, "layer", ("train", "query"), None, None),
        P(None, "layer", ("train", "query"), None, None),
        P(None, "layer", ("train", "query"), None, None),
        P(None, "layer", ("train", "query"), None, None),
        P("layer", None, None),
        P("layer", None, None),
        P(None, "layer", ("train", "query")),
        P(("train", "query")),
        P(("train", "query")),
    )
    out_specs = P("train", "query")
    return jax.shard_map(
        on_device, mesh=mesh, in_specs=in_specs, out_specs=out_specs, check_vma=False
    )
```

profile of v0, /device:TPU:8, one launch (start us, length us, event | category | flops | bytes accessed | tf_op | source)
XLA Modules:
  0.0 762.3 jit_solution(9087611071933525333)
XLA Ops:
  6.5 0.0 copy-start
  6.5 0.0 copy-start.1
  6.5 0.0 all-reduce.5.cloned.1.call-start
  7.4 0.8 copy-done
  8.1 1.8 fusion.29
  9.9 0.0 copy-done.1
  10.0 2.4 fusion.18
  12.4 0.7 reshape.48
  13.0 0.0 all-reduce.5.cloned.1.call-update
  13.1 0.0 all-reduce.7.cloned.1.call-start
  13.8 2.4 fusion.26
  16.2 2.4 fusion.15
  18.6 0.0 copy-start.2
  18.6 0.7 reshape.49
  19.3 36.3 %all-reduce.5.cloned.1.call-done = f32[2,1,8192]{2,0,1:T(2,128)} async-done(((f32[2,1,8192]{2,0,1:T(2,128)}), f32[2,1,8192]{2,0,1:T(2,128)}) %all-reduce.5.cloned.1.call-update) | async-done | bytes 65552 | tf_op jit(solution)/shard_map/psum | solution.py:55
  55.6 0.7 fusion.41
  56.3 183.9 %all_gather.6 = bf16[2,64,2048]{2,0,1:T(2,128)(2,1)S(1)} all-gather(bf16[2,1,2048]{2,0,1:T(2,128)(2,1)S(1)} %fusion.41), channel_id=1, replica_groups=mesh['layer'=4,'train'=8,'query'=8] {'train','query'}, dimensions={1}, use_global_device_ids=true | all-gather | bytes 532480 | tf_op jit(solution)/shard_map/all_gather | solution.py:66
  240.2 2.3 fusion.38
  242.5 0.0 all-reduce.7.cloned.1.call-update
  242.6 0.0 all-gather.2.cloned.1.call-start
  242.6 32.7 %all-reduce.7.cloned.1.call-done = (f32[2,64,128]{2,1,0:T(8,128)}, f32[2,1,8192]{2,0,1:T(2,128)}) async-done(((f32[2,64,128]{2,1,0:T(8,128)}, f32[2,1,8192]{2,0,1:T(2,128)}), (f32[2,64,128]{2,1,0:T(8,128)}, f32[2,1,8192]{2,0,1:T(2,128)})) %all-reduce.7.cloned.1.call-update) | async-done | bytes 131088 | tf_op jit(solution)/shard_map/psum | solution.py:73
  275.3 1.5 multiply_convert_fusion
  276.8 0.0 all-gather.2.cloned.1.call-update
  276.8 0.0 copy-done.2
  276.8 0.6 dynamic-slice
  278.0 119.7 %all-gather.2.cloned.1.call-done = bf16[2,64,8192]{2,0,1:T(2,128)(2,1)} async-done(((bf16[2,1,8192]{2,0,1:T(2,128)(2,1)}), bf16[2,64,8192]{2,0,1:T(2,128)(2,1)}) %all-gather.2.cloned.1.call-update) | async-done | bytes 2097168 | tf_op jit(solution)/shard_map/all_gather | solution.py:67
  397.7 0.8 constant_dynamic-slice_fusion.1
  398.5 1.0 convolution_bitcast_fusion
  399.5 0.1 reshape.50
  399.7 355.5 %all-reduce = f32[512,8]{1,0:T(8,128)S(1)} all-reduce(f32[512,8]{1,0:T(8,128)S(1)} %bitcast.56), channel_id=2, replica_groups=mesh['layer'=4,'train'=8,'query'=8] {'train','query'}, use_global_device_ids=true, to_apply=%region_3.4.clone | all-reduce | flops 4096 | bytes 32768
  755.2 0.6 constant_dynamic-slice_fusion
  (3 shorter events, 0.1 us)
Async XLA Ops:
  6.5 1.6 copy-start
  6.5 3.4 copy-start.1
  6.5 49.0 %all-reduce.5.cloned.1.call-start = ((), (), s32[]{:S(2)}) async-start(), calls=%async_computation | async-start | bytes 131072 | tf_op jit(solution)/shard_map/psum | solution.py:55
  13.1 262.2 %all-reduce.7.cloned.1.call-start = ((), (), s32[]{:S(2)}) async-start(), calls=%async_computation.2 | async-start | bytes 262144 | tf_op jit(solution)/shard_map/psum | solution.py:73
  18.6 258.2 %copy-start.2 = (u32[256]{0:T(256)S(1)}, u32[256]{0:T(256)}, u32[]{:S(2)}) copy-start(u32[256]{0:T(256)} %constant.38) | copy-start | bytes 3076
  242.6 155.2 %all-gather.2.cloned.1.call-start = ((), (), s32[]{:S(2)}) async-start(), calls=%async_computation.1 | async-start | bytes 2129920 | tf_op jit(solution)/shard_map/all_gather | solution.py:67
Sparse Core Ops, SparseCore 0:
  13.2 42.3 all-reduce.4
  242.7 32.5 all-reduce.6
  279.0 118.6 all-gather.1
where the time goes:
time: 763 us; the launch traced here: 762 us
  blocking collectives  539 us (71%)
  waiting for transfers between devices  189 us (25%)
  between operations  15.3 us (2%)
  matrix products  12.4 us (2%)
    unnamed x1, blocking collectives  355 us
    all_gather x1, blocking collectives, on_device(): lax.all_gather(train_block, ('train', 'query'), axis=1, tiled=True)  184 us
    all_gather x1, waiting for transfers between devices, on_device(): lax.all_gather(query_full, ('train', 'query'), axis=1, tiled=True)  120 us
    psum x1, waiting for transfers between devices, on_device(): train_total, query_total = lax.psum((train_terms, query_terms), 'layer')  36.3 us
    psum x1, waiting for transfers between devices, on_device(): preconditioned = lax.psum(partial_pre, 'layer')  32.7 us
  transfers between devices with their start and end apart: 3, of which 3 were waited for; matrix products, arithmetic and copies ran while one was open for 1% of the time, Pallas kernels for 0%

commit v1 on v0

v1 whole, which is shorter than its diff:
```python
import jax
import jax.numpy as jnp
from jax import lax
from jax.sharding import PartitionSpec as P


def sketch(activations, gradients, in_projection, out_projection, lengths):
    ckpt_count, _, row_count, seq_len, width = activations.shape
    positions = lax.broadcasted_iota(jnp.int32, (row_count, seq_len), 1)
    keep_mask = (positions < lengths[:, None]).reshape(1, row_count * seq_len, 1)
    flat_act = activations.reshape(ckpt_count, row_count * seq_len, width)
    flat_grad = gradients.reshape(ckpt_count, row_count * seq_len, width)
    inner = jnp.einsum(
        "cnd,dk->cnk", flat_act, in_projection[0], preferred_element_type=jnp.float32
    ).astype(jnp.bfloat16)
    outer = jnp.einsum(
        "cnd,dk->cnk", flat_grad, out_projection[0], preferred_element_type=jnp.float32
    )
    outer = jnp.where(keep_mask, outer, 0.0).astype(jnp.bfloat16)
    return jnp.einsum("cso,csi->coi", outer, inner, preferred_element_type=jnp.float32)


def on_device(
    train_act,
    train_grad,
    query_act,
    query_grad,
    in_projection,
    out_projection,
    inverse_hessian,
    train_lengths,
    query_lengths,
):
    seq_len = train_act.shape[3]
    layers = lax.axis_size("layer")
    rows_a, cols_b = lax.axis_size("train"), lax.axis_size("query")
    grid = rows_a * cols_b
    train_terms = sketch(train_act, train_grad, in_projection, out_projection, train_lengths)
    query_terms = sketch(query_act, query_grad, in_projection, out_projection, query_lengths)
    both = lax.all_gather(jnp.stack([train_terms, query_terms]), "layer")
    features = (jnp.sum(both, axis=0) / seq_len).astype(jnp.bfloat16)
    ckpts, outs, ins = train_terms.shape
    block = outs // layers
    layer_index = lax.axis_index("layer")
    train_block = lax.dynamic_slice_in_dim(features[0], layer_index * block, block, 1)
    train_message = jnp.broadcast_to(train_block[None], (grid, ckpts, block, ins))
    query_message = jnp.transpose(features[1], (1, 0, 2))[:, :, None, :]
    message = jnp.concatenate([train_message, query_message], axis=2)
    received = lax.all_to_all(message, ("train", "query"), 0, 0)
    train_rows = received[:, :, :block]
    query_columns = received[:, :, block]
    hessian = inverse_hessian.reshape(ckpts, block, ins, -1)
    partial_pre = jnp.einsum(
        "tcki,ckin->ctn", train_rows, hessian, preferred_element_type=jnp.float32
    )
    terms = jnp.einsum(
        "ctn,qcn->tq",
        partial_pre,
        query_columns.astype(jnp.float32),
        precision=lax.Precision.HIGHEST,
        preferred_element_type=jnp.float32,
    )
    tile_rows = terms.shape[0] // rows_a
    tile_cols = terms.shape[1] // cols_b
    tiles = terms.reshape(rows_a, tile_rows, cols_b, tile_cols)
    tiles = jnp.transpose(tiles, (0, 2, 1, 3)).reshape(1, grid, 1, tile_rows * tile_cols)
    tiles = jnp.broadcast_to(tiles, (layers, grid, 1, tile_rows * tile_cols))
    tiles = tiles.reshape(layers * grid, 1, tile_rows * tile_cols)
    shares = lax.all_to_all(tiles, ("layer", "train", "query"), 0, 0)
    return jnp.sum(shares, axis=0).reshape(tile_rows, tile_cols)


def solution(mesh):
    tokens = P(None, "layer", ("train", "query"), None, None)
    in_specs = (
        tokens,
        tokens,
        tokens,
        tokens,
        P("layer", None, None),
        P("layer", None, None),
        P(None, "layer", ("train", "query")),
        P(("train", "query")),
        P(("train", "query")),
    )
    return jax.shard_map(
        on_device, mesh=mesh, in_specs=in_specs, out_specs=P("train", "query"), check_vma=False
    )
```

time: 763 us -> 74.7 us (0.10)
  the two profiles are of different devices: /device:TPU:8 before, /device:TPU:1 now
where the time goes in v1:
time: 74.7 us; the launch traced here: 74.5 us
  blocking collectives  61.5 us (82%)
  matrix products  8.3 us (11%)
  between operations  2.03 us (3%)
  local copies, waits for them, and re-layouts  1.56 us (2%)
  other arithmetic  1.09 us (1%)
    all_to_all x1, blocking collectives, on_device(): received = lax.all_to_all(message, ('train', 'query'), 0, 0)  31.6 us
    all_to_all x1, blocking collectives, on_device(): shares = lax.all_to_all(tiles, ('layer', 'train', 'query'), 0, 0)  20.3 us
    all_gather x1, blocking collectives, on_device(): both = lax.all_gather(jnp.stack([train_terms, query_terms]), 'layer')  9.59 us
    dot_general x2, matrix products, sketch(): jnp.einsum('cso,csi->coi', outer, inner, preferred_element_type=jnp.float32)  4.81 us
    dot_general x2, matrix products, sketch(): jnp.einsum('cnd,dk->cnk', flat_grad, out_projection[0], preferred_element...  2.66 us

profile of v1, /device:TPU:1, one launch (start us, length us, event | category | flops | bytes accessed | tf_op | source)
XLA Modules:
  0.0 74.5 jit_solution(11969133116633745046)
XLA Ops:
  0.0 0.0 copy-start
  0.0 0.0 copy-start.2
  0.0 0.0 copy-start.3
  1.9 0.0 copy-done
  1.9 0.0 copy-start.1
  1.9 1.9 %fusion.35 = bf16[2,128,64]{1,2,0:T(8,128)(2,1)S(1)} fusion(bf16[2,1,1,128,4096]{4,3,2,1,0:T(8,128)(2,1)S(1)} %copy-done, bf16[1,4096,64]{1,2,0:T(8,128)(2,1)} %param.14, pred[128]{0:T(512)(128)(4,1)S(1)} %iota_compare_fusion.1), kind=kOutput, calls=%fused_computation.19 | convolution fusion | flops 134250496 | bytes 2654336 | tf_op jit(solution)/shard_map/cnd,dk->cnk/dot_general | solution.py:16
  3.8 0.0 copy-done.2
  3.8 0.0 copy-done.3
  3.8 0.8 %fusion.32 = bf16[2,128,64]{1,2,0:T(8,128)(2,1)S(1)} fusion(bf16[2,1,1,128,4096]{4,3,2,1,0:T(8,128)(2,1)S(1)} %copy-done.2, bf16[1,4096,64]{1,2,0:T(8,128)(2,1)S(1)} %copy-done.3, pred[128]{0:T(512)(128)(4,1)S(1)} %iota_compare_fusion), kind=kOutput, calls=%fused_computation.18 | convolution fusion | flops 134250496 | bytes 2654336 | tf_op jit(solution)/shard_map/cnd,dk->cnk/dot_general | solution.py:16
  4.6 0.0 copy-done.1
  4.6 2.4 %fusion.17 = f32[1,2,64,128]{3,2,1,0:T(8,128)S(1)} fusion(bf16[2,128,64]{1,2,0:T(8,128)(2,1)S(1)} %fusion.32, bf16[2,1,1,128,4096]{4,3,2,1,0:T(8,128)(2,1)} %param.11, bf16[1,4096,128]{2,1,0:T(8,128)(2,1)S(1)} %copy-done.1), kind=kOutput, calls=%fused_computation.13 | convolution fusion | flops 272662528 | bytes 3244032 | tf_op jit(solution)/shard_map/cso,csi->coi/dot_general | solution.py:20
  7.0 2.4 %fusion.23 = f32[1,2,64,128]{3,2,1,0:T(8,128)S(1)} fusion(bf16[2,128,64]{1,2,0:T(8,128)(2,1)S(1)} %fusion.35, bf16[2,1,1,128,4096]{4,3,2,1,0:T(8,128)(2,1)} %param.9, bf16[1,4096,128]{2,1,0:T(8,128)(2,1)S(1)} %copy-done.1), kind=kOutput, calls=%fused_computation.15 | convolution fusion | flops 272662528 | bytes 3244032 | tf_op jit(solution)/shard_map/cso,csi->coi/dot_general | solution.py:20
  9.4 9.6 %all-gather = f32[8,2,64,128]{3,2,1,0:T(8,128)S(1)} all-gather(f32[2,2,64,128]{3,2,1,0:T(8,128)S(1)} %pad_maximum_fusion.1), channel_id=2, replica_groups=mesh['layer'=4,'train'=8,'query'=8] {'layer'}, dimensions={0}, use_global_device_ids=true | all-gather | bytes 655360 | tf_op jit(solution)/shard_map/all_gather | solution.py:40
  19.0 0.0 copy-start.4
  19.2 0.3 broadcast_in_dim.44
  19.5 0.7 pad_maximum_fusion
  20.2 31.6 %all_to_all.10 = bf16[64,2,17,128]{3,1,2,0:T(2,128)(2,1)S(1)} all-to-all(bf16[64,2,17,128]{3,1,2,0:T(2,128)(2,1)S(1)} %pad_maximum_fusion), channel_id=1, replica_groups=mesh['layer'=4,'train'=8,'query'=8] {'train','query'}, dimensions={0} | all-to-all | bytes 1114112 | tf_op jit(solution)/shard_map/all_to_all | solution.py:49
  51.8 0.4 slice.18
  52.1 0.0 copy-done.4
  52.1 0.4 convolution_bitcast_fusion.1
  52.6 0.4 convolution_bitcast_fusion
  53.0 0.1 broadcast_in_dim.46
  53.2 20.3 %all_to_all.11 = f32[256,1,64]{2,1,0:T(1,128)S(1)} all-to-all(f32[256,1,64]{2,1,0:T(1,128)S(1)} %bitcast.93), channel_id=1, replica_groups=mesh['layer'=4,'train'=8,'query'=8] {'layer','train','query'}, dimensions={0} | all-to-all | bytes 131072 | tf_op jit(solution)/shard_map/all_to_all | solution.py:69
  73.5 0.3 reduce_sum.19
  73.8 0.7 reshape.59
  (11 shorter events, 0.2 us)
Async XLA Ops:
  0.0 1.9 %copy-start = (bf16[2,1,1,128,4096]{4,3,2,1,0:T(8,128)(2,1)S(1)}, bf16[2,1,1,128,4096]{4,3,2,1,0:T(8,128)(2,1)}, u32[]{:S(2)}) copy-start(bf16[2,1,1,128,4096]{4,3,2,1,0:T(8,128)(2,1)} %param.10) | copy-start | bytes 6291460
  0.0 3.8 %copy-start.2 = (bf16[2,1,1,128,4096]{4,3,2,1,0:T(8,128)(2,1)S(1)}, bf16[2,1,1,128,4096]{4,3,2,1,0:T(8,128)(2,1)}, u32[]{:S(2)}) copy-start(bf16[2,1,1,128,4096]{4,3,2,1,0:T(8,128)(2,1)} %param.12) | copy-start | bytes 6291460
  0.0 3.8 %copy-start.3 = (bf16[1,4096,64]{1,2,0:T(8,128)(2,1)S(1)}, bf16[1,4096,64]{1,2,0:T(8,128)(2,1)}, u32[]{:S(2)}) copy-start(bf16[1,4096,64]{1,2,0:T(8,128)(2,1)} %param.14) | copy-start | bytes 1572868
  1.9 2.7 %copy-start.1 = (bf16[1,4096,128]{2,1,0:T(8,128)(2,1)S(1)}, bf16[1,4096,128]{2,1,0:T(8,128)(2,1)}, u32[]{:S(2)}) copy-start(bf16[1,4096,128]{2,1,0:T(8,128)(2,1)} %param.13) | copy-start | bytes 3145732
  19.0 33.1 %copy-start.4 = (bf16[2,2048,128]{2,1,0:T(8,128)(2,1)S(1)}, bf16[2,2048,128]{2,1,0:T(8,128)(2,1)}, u32[]{:S(2)}) copy-start(bf16[2,2048,128]{2,1,0:T(8,128)(2,1)} %param.15) | copy-start | bytes 3145732

commit v2 on v1

v2 whole, which is shorter than its diff:
```python
import jax
import jax.numpy as jnp
from jax import lax
from jax.experimental import pallas as pl
from jax.experimental.pallas import tpu as pltpu
from jax.sharding import PartitionSpec as P

CHUNKS = 4
AHEAD = 3


def sketch_kernel(
    train_length,
    query_length,
    train_act,
    train_grad,
    query_act,
    query_grad,
    in_projection,
    out_projection,
    result,
    act,
    grad,
    in_weights,
    out_weights,
    inner,
    outer,
    arrived,
):
    ckpts, seq_len, width = train_act.shape
    chunk = width // CHUNKS
    rows = 2 * ckpts * seq_len
    copies = []
    for step in range(CHUNKS):
        cols = pl.ds(step * chunk, chunk)
        group = [
            (in_projection.at[cols], in_weights.at[cols]),
            (train_act.at[:, :, cols], act.at[pl.ds(0, ckpts), :, cols]),
            (query_act.at[:, :, cols], act.at[pl.ds(ckpts, ckpts), :, cols]),
            (out_projection.at[:, cols], out_weights.at[:, cols]),
            (train_grad.at[:, :, cols], grad.at[pl.ds(0, ckpts), :, cols]),
            (query_grad.at[:, :, cols], grad.at[pl.ds(ckpts, ckpts), :, cols]),
        ]
        group = [
            pltpu.make_async_copy(source, target, arrived.at[step, place])
            for place, (source, target) in enumerate(group)
        ]
        copies.append(group)
    for group in copies[:AHEAD]:
        for copy in group:
            copy.start()
    for step, group in enumerate(copies):
        cols = pl.ds(step * chunk, chunk)
        for copy in group:
            copy.wait()
        for ahead in copies[step + AHEAD : step + AHEAD + 1]:
            for copy in ahead:
                copy.start()
        inner_term = jnp.dot(
            act[:, :, cols].reshape(rows, chunk),
            in_weights[cols],
            preferred_element_type=jnp.float32,
        )
        outer_term = lax.dot_general(
            grad[:, :, cols].reshape(rows, chunk),
            out_weights[:, cols],
            (((1,), (1,)), ((), ())),
            preferred_element_type=jnp.float32,
        )
        if step == 0:
            inner[...] = inner_term
            outer[...] = outer_term
        else:
            inner[...] += inner_term
            outer[...] += outer_term
    for side, length in enumerate((train_length, query_length)):
        for ckpt in range(ckpts):
            part = pl.ds((side * ckpts + ckpt) * seq_len, seq_len)
            kept = outer[part]
            positions = lax.broadcasted_iota(jnp.int32, kept.shape, 0)
            kept = jnp.where(positions < length[0], kept, 0.0).astype(jnp.bfloat16)
            total = lax.dot_general(
                kept,
                inner[part].astype(jnp.bfloat16),
                (((0,), (0,)), ((), ())),
                preferred_element_type=jnp.float32,
            )
            result[side, ckpt] = total.astype(result.dtype)


def sketches(train_act, train_grad, query_act, query_grad, in_projection, out_projection, train_length, query_length):
    ckpts, _, _, seq_len, width = train_act.shape
    ins, outs = in_projection.shape[2], out_projection.shape[2]
    flat = [x.reshape(ckpts, seq_len, width) for x in (train_act, train_grad, query_act, query_grad)]
    stay = pl.BlockSpec(memory_space=pl.ANY)
    scalar = pl.BlockSpec(memory_space=pltpu.SMEM)
    rows = 2 * ckpts * seq_len
    return pl.pallas_call(
        sketch_kernel,
        out_shape=jax.ShapeDtypeStruct((2, ckpts, outs, ins), jnp.bfloat16),
        in_specs=[scalar, scalar] + [stay] * 6,
        out_specs=pl.BlockSpec(memory_space=pltpu.VMEM),
        scratch_shapes=[
            pltpu.VMEM((2 * ckpts, seq_len, width), jnp.bfloat16),
            pltpu.VMEM((2 * ckpts, seq_len, width), jnp.bfloat16),
            pltpu.VMEM((width, ins), jnp.bfloat16),
            pltpu.VMEM((outs, width), jnp.bfloat16),
            pltpu.VMEM((rows, ins), jnp.float32),
            pltpu.VMEM((rows, outs), jnp.float32),
            pltpu.SemaphoreType.DMA((CHUNKS, 6)),
        ],
        compiler_params=pltpu.CompilerParams(vmem_limit_bytes=60 * 1024 * 1024),
        name="sketches",
    )(train_length, query_length, *flat, in_projection[0], out_projection[0].T)


def on_device(
    train_act,
    train_grad,
    query_act,
    query_grad,
    in_projection,
    out_projection,
    inverse_hessian,
    train_lengths,
    query_lengths,
):
    seq_len = train_act.shape[3]
    layers = lax.axis_size("layer")
    rows_a, cols_b = lax.axis_size("train"), lax.axis_size("query")
    grid = rows_a * cols_b
    terms = sketches(
        train_act, train_grad, query_act, query_grad, in_projection, out_projection, train_lengths, query_lengths
    )
    _, ckpts, outs, ins = terms.shape
    block = outs // layers
    half = block // 2
    pairs = cols_b // 2
    parity = lax.rem(lax.axis_index("query"), 2)
    hessian = inverse_hessian.reshape(ckpts, 2, half, ins, -1)
    other_half = lax.dynamic_index_in_dim(hessian, 1 - parity, 1, keepdims=False)
    swap = [(i, i ^ 1) for i in range(cols_b)]
    hessian_other = lax.ppermute(other_half, "query", swap)
    hessian_own = lax.dynamic_index_in_dim(hessian, parity, 1, keepdims=False)
    layer_index = lax.axis_index("layer")
    gathered = lax.all_gather(terms, "layer")
    total = jnp.sum(gathered.astype(jnp.float32), axis=0) / seq_len
    features = jnp.concatenate(
        [lax.dynamic_slice_in_dim(total[0], layer_index * block, block, 1), total[1]], axis=1
    ).astype(jnp.bfloat16)
    train_block = jnp.transpose(features[:, :block].reshape(ckpts, 2, half, ins), (1, 2, 0, 3))
    train_message = jnp.broadcast_to(train_block[None, :, None], (pairs, 2, rows_a, half, ckpts, ins))
    train_message = train_message.reshape(grid, half, ckpts, ins)
    query = features[:, block:].reshape(ckpts, rows_a, pairs, 2, ins)
    query_own = jnp.transpose(query, (2, 3, 1, 0, 4)).reshape(grid, 1, ckpts, ins)
    query_other = jnp.transpose(jnp.flip(query, 3), (2, 3, 1, 0, 4)).reshape(grid, 1, ckpts, ins)
    message = jnp.concatenate([train_message, query_own, query_other], axis=1)
    message, hessian_other = lax.optimization_barrier((message, hessian_other))
    received = lax.all_to_all(message, ("query", "train"), 0, 0)
    train_rows = received[:, :half]
    query_columns = jnp.concatenate([received[:, half], received[:, half + 1]], axis=2)
    partial_pre = jnp.concatenate(
        [
            jnp.einsum("tkci,ckin->ctn", train_rows, part, preferred_element_type=jnp.float32)
            for part in (hessian_own, hessian_other)
        ],
        axis=2,
    )
    scores = jnp.einsum(
        "ctn,qcn->tq",
        partial_pre,
        query_columns.astype(jnp.float32),
        precision=lax.Precision.HIGHEST,
        preferred_element_type=jnp.float32,
    )
    tile_rows = scores.shape[0] // rows_a
    tile_cols = scores.shape[1] // cols_b
    tiles = scores.reshape(cols_b, rows_a, tile_cols, cols_b)
    tiles = jnp.transpose(tiles, (1, 3, 0, 2)).reshape(1, grid, 1, tile_rows * tile_cols)
    tiles = jnp.broadcast_to(tiles, (layers, grid, 1, tile_rows * tile_cols))
    tiles = tiles.reshape(layers * grid, 1, tile_rows * tile_cols)
    shares = lax.all_to_all(tiles, ("layer", "train", "query"), 0, 0)
    return jnp.sum(shares, axis=0).reshape(tile_rows, tile_cols)


def solution(mesh):
    tokens = P(None, "layer", ("train", "query"), None, None)
    in_specs = (
        tokens,
        tokens,
        tokens,
        tokens,
        P("layer", None, None),
        P("layer", None, None),
        P(None, "layer", ("train", "query")),
        P(("train", "query")),
        P(("train", "query")),
    )
    return jax.shard_map(
        on_device, mesh=mesh, in_specs=in_specs, out_specs=P("train", "query"), check_vma=False
    )
```

time: 74.7 us -> 68.7 us (0.920)
  matrix products: 8.3 us -> 0.65 us
  blocking collectives: 61.5 us -> 54.1 us
  Pallas kernels: 0 us -> 5.81 us
  starting transfers between devices: 0 us -> 2.55 us
  local copies, waits for them, and re-layouts: 1.56 us -> 3.05 us
    dot_general x5 -> x2, matrix products: 7.91 us -> 0.45 us  [on_device(): jnp.einsum('tkci,ckin->ctn', train_rows, part, preferred_element_type=jnp...]
    pallas_call x0 -> x1, Pallas kernels: none -> 5.81 us  [sketches(): pl.pallas_call(sketch_kernel, out_shape=jax.ShapeDtypeStruct((2, ckpts, o...]
    all_to_all x1, blocking collectives: 31.6 us -> 26.4 us  [on_device(): received = lax.all_to_all(message, ('query', 'train'), 0, 0)]
    all_gather x1, blocking collectives: 9.59 us -> 6.83 us  [on_device(): gathered = lax.all_gather(terms, 'layer')]
    ppermute x0 -> x1, starting transfers between devices: none -> 2.55 us  [on_device(): hessian_other = lax.ppermute(other_half, 'query', swap)]
    dynamic_slice x0 -> x2, local copies, waits for them, and re-layouts: none -> 1.31 us  [the longest x1 1.27 us: on_device(): hessian_own = lax.dynamic_index_in_dim(hessian, parity, 1, keepdims=False)]
  transfers between devices with their start and end apart: 0 -> 1, of which waited for: 0 -> 0; matrix products, arithmetic and copies ran while one was open for 0% -> 1% of each run, Pallas kernels for 0% -> 8%
where the time goes in v2:
time: 68.7 us; the launch traced here: 68.5 us
  blocking collectives  54.1 us (79%)
  Pallas kernels  5.81 us (8%)
  local copies, waits for them, and re-layouts  3.05 us (4%)
  starting transfers between devices  2.55 us (4%)
  between operations  1.48 us (2%)
  other arithmetic  0.81 us (1%)
    all_to_all x1, blocking collectives, on_device(): received = lax.all_to_all(message, ('query', 'train'), 0, 0)  26.4 us
    all_to_all x1, blocking collectives, on_device(): shares = lax.all_to_all(tiles, ('layer', 'train', 'query'), 0, 0)  20.9 us
    all_gather x1, blocking collectives, on_device(): gathered = lax.all_gather(terms, 'layer')  6.83 us
    pallas_call x1, Pallas kernels, sketches(): pl.pallas_call(sketch_kernel, out_shape=jax.ShapeDtypeStruct((2, ckpts, o...  5.81 us
    ppermute x1, starting transfers between devices, on_device(): hessian_other = lax.ppermute(other_half, 'query', swap)  2.55 us
  transfers between devices with their start and end apart: 1, of which 0 were waited for; matrix products, arithmetic and copies ran while one was open for 1% of the time, Pallas kernels for 8%

profile of v2, /device:TPU:1, one launch (start us, length us, event | category | flops | bytes accessed | tf_op | source)
XLA Modules:
  0.0 68.5 jit_solution(8789692905360022128)
XLA Ops:
  0.0 1.3 %constant_dynamic-slice_fusion = (bf16[2,1,8,128,128]{4,3,2,1,0:T(8,128)(2,1)S(1)}, bf16[2,1,8,128,128]{4,3,2,1,0:T(8,128)(2,1)S(1)}) fusion(bf16[2,2,8,128,128]{4,3,2,1,0:T(8,128)(2,1)} %bitcast.50, s32[]{:T(128)S(6)} %select_n.12, s32[]{:T(128)S(6)} %select_n.11), kind=kLoop, calls=%fused_computation.21 | loop fusion | bytes 2097160 | tf_op jit(solution)/shard_map/jit(dynamic_index_in_dim)/dynamic_slice | solution.py:144
  1.3 2.6 %collective-permute-start = (bf16[2,8,128,128]{3,2,0,1:T(8,128)(2,1)S(1)}, bf16[2,8,128,128]{3,2,0,1:T(8,128)(2,1)S(1)}, u32[]{:S(2)}, u32[]{:S(2)}) collective-permute-start(bf16[2,8,128,128]{3,2,0,1:T(8,128)(2,1)S(1)} %bitcast.53), channel_id=1, source_target_pairs={{0,1},{1,0},{2,3},{3,2},{4,5},{5,4},{6,7},{7,6},{8,9},{9,8},{10,11... | collective-permute-start | bytes 1572872 | tf_op jit(solution)/shard_map/ppermute | solution.py:143
  5.2 5.8 %sketches.1 = bf16[2,2,64,128]{3,2,1,0:T(8,128)(2,1)} custom-call(s32[1]{0:T(128)S(6)} %copy.46.train_length, s32[1]{0:T(128)S(6)} %copy.47.query_length, bf16[2,128,4096]{2,1,0:T(8,128)(2,1)} %bitcast.43, bf16[2,128,4096]{2,1,0:T(8,128)(2,1)} %bitcast.44, bf16[2,128,4096]{2,1,0:T(8,128)(2,1)} %bitcast.45, bf16[2,128,4096]{2,1,0:T(8,128)(2,1)} %bitcast.46, ...), custom_call_target="tpu_custom_call" | custom-call | tf_op jit(solution)/shard_map/sketches/pallas_call | solution.py:98
  11.0 6.8 %all-gather = bf16[8,2,64,128]{3,2,1,0:T(8,128)(2,1)S(1)} all-gather(bf16[2,2,64,128]{3,2,1,0:T(8,128)(2,1)} %sketches.1), channel_id=2, replica_groups=mesh['layer'=4,'train'=8,'query'=8] {'layer'}, dimensions={0}, use_global_device_ids=true | all-gather | bytes 327680 | tf_op jit(solution)/shard_map/all_gather | solution.py:146
  17.9 0.2 rev.4
  18.2 0.1 broadcast_in_dim.15
  18.4 0.5 pad_maximum_fusion
  18.8 0.0 collective-permute-done
  18.9 26.4 %all_to_all.10 = bf16[64,10,2,128]{3,2,1,0:T(2,128)(2,1)S(1)} all-to-all(bf16[64,10,2,128]{3,2,1,0:T(2,128)(2,1)S(1)} %pad_maximum_fusion), channel_id=1, replica_groups=mesh['layer'=4,'train'=8,'query'=8] {'query','train'}, dimensions={0} | all-to-all | bytes 655360 | tf_op jit(solution)/shard_map/all_to_all | solution.py:159
  45.2 0.2 slice.25
  45.4 0.2 convolution_bitcast_fusion.1
  45.6 0.2 convolution_bitcast_fusion
  45.9 0.2 convolution_bitcast_fusion.2
  46.2 0.1 reshape.61
  46.3 0.1 copy.31
  46.4 0.1 broadcast_in_dim.16
  46.6 20.9 %all_to_all.11 = f32[256,1,64]{2,1,0:T(1,128)S(1)} all-to-all(f32[256,1,64]{2,1,0:T(1,128)S(1)} %bitcast.52), channel_id=1, replica_groups=mesh['layer'=4,'train'=8,'query'=8] {'layer','train','query'}, dimensions={0} | all-to-all | bytes 131072 | tf_op jit(solution)/shard_map/all_to_all | solution.py:182
  67.5 0.3 reduce_sum.19
  67.8 0.7 reshape.62
  (13 shorter events, 0.3 us)
Async XLA Ops:
  1.3 17.5 %collective-permute-start = (bf16[2,8,128,128]{3,2,0,1:T(8,128)(2,1)S(1)}, bf16[2,8,128,128]{3,2,0,1:T(8,128)(2,1)S(1)}, u32[]{:S(2)}, u32[]{:S(2)}) collective-permute-start(bf16[2,8,128,128]{3,2,0,1:T(8,128)(2,1)S(1)} %bitcast.53), channel_id=1, source_target_pairs={{0,1},{1,0},{2,3},{3,2},{4,5},{5,4},{6,7},{7,6},{8,9},{9,8},{10,11... | collective-permute-start | bytes 1572872 | tf_op jit(solution)/shard_map/ppermute | solution.py:143

commit v3 on v2

--- a/solution.py
+++ b/solution.py
@@ -85,7 +85,7 @@
                 (((0,), (0,)), ((), ())),
                 preferred_element_type=jnp.float32,
             )
-            result[side, ckpt] = total.astype(result.dtype)
+            result[side, ckpt] = total
 
 
 def sketches(train_act, train_grad, query_act, query_grad, in_projection, out_projection, train_length, query_length):
@@ -97,7 +97,7 @@
     rows = 2 * ckpts * seq_len
     return pl.pallas_call(
         sketch_kernel,
-        out_shape=jax.ShapeDtypeStruct((2, ckpts, outs, ins), jnp.bfloat16),
+        out_shape=jax.ShapeDtypeStruct((2, ckpts, outs, ins), jnp.float32),
         in_specs=[scalar, scalar] + [stay] * 6,
         out_specs=pl.BlockSpec(memory_space=pltpu.VMEM),
         scratch_shapes=[
@@ -112,6 +112,13 @@
         compiler_params=pltpu.CompilerParams(vmem_limit_bytes=60 * 1024 * 1024),
         name="sketches",
     )(train_length, query_length, *flat, in_projection[0], out_projection[0].T)
+
+
+def add_shares(shares, tile):
+    total = jnp.sum(shares[...], axis=0, keepdims=True)
+    width = tile.shape[1]
+    for row in range(tile.shape[0]):
+        tile[pl.ds(row, 1)] = total[:, row * width : (row + 1) * width]
 
 
 def on_device(
@@ -135,25 +142,30 @@
     _, ckpts, outs, ins = terms.shape
     block = outs // layers
     half = block // 2
-    pairs = cols_b // 2
-    parity = lax.rem(lax.axis_index("query"), 2)
+    pairs = rows_a // 2
+    parity = lax.rem(lax.axis_index("train"), 2)
     hessian = inverse_hessian.reshape(ckpts, 2, half, ins, -1)
     other_half = lax.dynamic_index_in_dim(hessian, 1 - parity, 1, keepdims=False)
-    swap = [(i, i ^ 1) for i in range(cols_b)]
-    hessian_other = lax.ppermute(other_half, "query", swap)
+    swap = [(i, i ^ 1) for i in range(rows_a)]
+    hessian_other = lax.ppermute(other_half, "train", swap)
     hessian_own = lax.dynamic_index_in_dim(hessian, parity, 1, keepdims=False)
     layer_index = lax.axis_index("layer")
-    gathered = lax.all_gather(terms, "layer")
-    total = jnp.sum(gathered.astype(jnp.float32), axis=0) / seq_len
-    features = jnp.concatenate(
-        [lax.dynamic_slice_in_dim(total[0], layer_index * block, block, 1), total[1]], axis=1
+    gathered = lax.all_gather(terms, "layer", axis_index_groups=[[i, i + 1] for i in range(0, layers, 2)])
+    terms = gathered[0] + gathered[1]
+    outgoing = jnp.concatenate(
+        [lax.dynamic_slice_in_dim(terms[0], (layer_index ^ 2) * block, block, 1), terms[1]], axis=1
     ).astype(jnp.bfloat16)
+    own = jnp.concatenate(
+        [lax.dynamic_slice_in_dim(terms[0], layer_index * block, block, 1), terms[1]], axis=1
+    )
+    incoming = lax.ppermute(outgoing, "layer", [(i, i ^ 2) for i in range(layers)])
+    features = ((own + incoming.astype(jnp.float32)) / seq_len).astype(jnp.bfloat16)
     train_block = jnp.transpose(features[:, :block].reshape(ckpts, 2, half, ins), (1, 2, 0, 3))
-    train_message = jnp.broadcast_to(train_block[None, :, None], (pairs, 2, rows_a, half, ckpts, ins))
+    train_message = jnp.broadcast_to(train_block, (cols_b, pairs, 2, half, ckpts, ins))
     train_message = train_message.reshape(grid, half, ckpts, ins)
-    query = features[:, block:].reshape(ckpts, rows_a, pairs, 2, ins)
-    query_own = jnp.transpose(query, (2, 3, 1, 0, 4)).reshape(grid, 1, ckpts, ins)
-    query_other = jnp.transpose(jnp.flip(query, 3), (2, 3, 1, 0, 4)).reshape(grid, 1, ckpts, ins)
+    query = features[:, block:].reshape(ckpts, pairs, 2, cols_b, ins)
+    query_own = jnp.transpose(query, (3, 1, 2, 0, 4)).reshape(grid, 1, ckpts, ins)
+    query_other = jnp.transpose(jnp.flip(query, 2), (3, 1, 2, 0, 4)).reshape(grid, 1, ckpts, ins)
     message = jnp.concatenate([train_message, query_own, query_other], axis=1)
     message, hessian_other = lax.optimization_barrier((message, hessian_other))
     received = lax.all_to_all(message, ("query", "train"), 0, 0)
@@ -180,7 +192,12 @@
     tiles = jnp.broadcast_to(tiles, (layers, grid, 1, tile_rows * tile_cols))
     tiles = tiles.reshape(layers * grid, 1, tile_rows * tile_cols)
     shares = lax.all_to_all(tiles, ("layer", "train", "query"), 0, 0)
-    return jnp.sum(shares, axis=0).reshape(tile_rows, tile_cols)
+    return pl.pallas_call(
+        add_shares,
+        out_shape=jax.ShapeDtypeStruct((tile_rows, tile_cols), jnp.float32),
+        compiler_params=pltpu.CompilerParams(vmem_limit_bytes=4 * 1024 * 1024),
+        name="add_shares",
+    )(shares.reshape(layers * grid, tile_rows * tile_cols))
 
 
 def solution(mesh):

time: 68.7 us -> 67.5 us (0.983)
  blocking collectives: 54.1 us -> 50.8 us
  waiting for transfers between devices: 0.01 us -> 1.81 us
  local copies, waits for them, and re-layouts: 3.05 us -> 2.27 us
  Pallas kernels: 5.81 us -> 6.54 us
  starting transfers between devices: 2.55 us -> 3.26 us
    all_gather x1, blocking collectives: 6.83 us -> 3.05 us  [on_device(): lax.all_gather(terms, 'layer', axis_index_groups=[[i, i + 1] for i in ran...]
    ppermute x1 -> x2, waiting for transfers between devices: 0.01 us -> 1.81 us  [the longest x1 1.81 us: on_device(): lax.ppermute(outgoing, 'layer', [(i, i ^ 2) for i in range(layers)])]
    all_to_all x1, blocking collectives: 20.9 us -> 21.9 us  [on_device(): shares = lax.all_to_all(tiles, ('layer', 'train', 'query'), 0, 0)]
    reshape x3 -> x0, local copies, waits for them, and re-layouts: 0.75 us -> none  [the longest x1 0.68 us: on_device(): return jnp.sum(shares, axis=0).reshape(tile_rows, tile_cols)]
    pallas_call x0 -> x1, Pallas kernels: none -> 0.71 us  [on_device(): pl.pallas_call(add_shares, out_shape=jax.ShapeDtypeStruct((tile_rows, til...]
    ppermute x1 -> x2, starting transfers between devices: 2.55 us -> 3.26 us  [the longest x1 2.13 us: on_device(): hessian_other = lax.ppermute(other_half, 'train', swap)]
  transfers between devices with their start and end apart: 1 -> 2, of which waited for: 0 -> 1; matrix products, arithmetic and copies ran while one was open for 1% -> 1% of each run, Pallas kernels for 8% -> 9%
where the time goes in v3:
time: 67.5 us; the launch traced here: 67.3 us
  blocking collectives  50.8 us (75%)
  Pallas kernels  6.54 us (10%)
  starting transfers between devices  3.26 us (5%)
  local copies, waits for them, and re-layouts  2.27 us (3%)
  waiting for transfers between devices  1.81 us (3%)
  between operations  1.51 us (2%)
    all_to_all x1, blocking collectives, on_device(): received = lax.all_to_all(message, ('query', 'train'), 0, 0)  25.8 us
    all_to_all x1, blocking collectives, on_device(): shares = lax.all_to_all(tiles, ('layer', 'train', 'query'), 0, 0)  21.9 us
    pallas_call x1, Pallas kernels, sketches(): pl.pallas_call(sketch_kernel, out_shape=jax.ShapeDtypeStruct((2, ckpts, o...  5.83 us
    all_gather x1, blocking collectives, on_device(): lax.all_gather(terms, 'layer', axis_index_groups=[[i, i + 1] for i in ran...  3.05 us
    ppermute x1, starting transfers between devices, on_device(): hessian_other = lax.ppermute(other_half, 'train', swap)  2.13 us
    ppermute x1, waiting for transfers between devices, on_device(): lax.ppermute(outgoing, 'layer', [(i, i ^ 2) for i in range(layers)])  1.81 us
  transfers between devices with their start and end apart: 2, of which 1 were waited for; matrix products, arithmetic and copies ran while one was open for 1% of the time, Pallas kernels for 9%

profile of v3, /device:TPU:1, one launch (start us, length us, event | category | flops | bytes accessed | tf_op | source)
XLA Modules:
  0.0 67.3 jit_solution(13127243864688147111)
XLA Ops:
  0.0 1.3 %constant_dynamic-slice_fusion = (bf16[2,1,8,128,128]{4,3,2,1,0:T(8,128)(2,1)S(1)}, bf16[2,1,8,128,128]{4,3,2,1,0:T(8,128)(2,1)S(1)}) fusion(bf16[2,2,8,128,128]{4,3,2,1,0:T(8,128)(2,1)} %bitcast.60, s32[]{:T(128)S(6)} %select_n.16, s32[]{:T(128)S(6)} %select_n.15), kind=kLoop, calls=%fused_computation.28 | loop fusion | bytes 2097160 | tf_op jit(solution)/shard_map/jit(dynamic_index_in_dim)/dynamic_slice | solution.py:151
  1.3 2.1 %collective-permute-start.1 = (bf16[2,8,128,128]{3,2,0,1:T(8,128)(2,1)S(1)}, bf16[2,8,128,128]{3,2,0,1:T(8,128)(2,1)S(1)}, u32[]{:S(2)}, u32[]{:S(2)}) collective-permute-start(bf16[2,8,128,128]{3,2,0,1:T(8,128)(2,1)S(1)} %bitcast.63), channel_id=1, source_target_pairs={{0,8},{8,0},{16,24},{24,16},{32,40},{40,32},{48,56},{56,48},{1,9},... | collective-permute-start | bytes 1572872 | tf_op jit(solution)/shard_map/ppermute | solution.py:150
  4.8 5.8 %sketches.1 = f32[2,2,64,128]{3,2,1,0:T(8,128)} custom-call(s32[1]{0:T(128)S(6)} %copy.40.train_length, s32[1]{0:T(128)S(6)} %copy.41.query_length, bf16[2,128,4096]{2,1,0:T(8,128)(2,1)} %bitcast.54, bf16[2,128,4096]{2,1,0:T(8,128)(2,1)} %bitcast.55, bf16[2,128,4096]{2,1,0:T(8,128)(2,1)} %bitcast.56, bf16[2,128,4096]{2,1,0:T(8,128)(2,1)} %bitcast.57, ...), custom_call_target="tpu_custom_call" | custom-call | tf_op jit(solution)/shard_map/sketches/pallas_call | solution.py:98
  10.6 3.1 %all-gather = f32[4,2,64,128]{3,2,1,0:T(8,128)S(1)} all-gather(f32[2,2,64,128]{3,2,1,0:T(8,128)} %sketches.1), channel_id=2, replica_groups={{0,64},{128,192},{1,65},{129,193},{2,66},{130,194},{3,67},{131,195},{4,..., dimensions={0}, use_global_device_ids=true | all-gather | bytes 393216 | tf_op jit(solution)/shard_map/all_gather | solution.py:153
  13.8 1.1 %collective-permute-start = (bf16[2,80,128]{2,1,0:T(8,128)(2,1)S(1)}, bf16[2,80,128]{2,1,0:T(8,128)(2,1)S(1)}, u32[]{:S(2)}, u32[]{:S(2)}) collective-permute-start(bf16[2,80,128]{2,1,0:T(8,128)(2,1)S(1)} %pad_maximum_fusion.1), channel_id=1, source_target_pairs={{0,128},{64,192},{128,0},{192,64},{1,129},{65,193},{129,1},{193,65... | collective-permute-start | bytes 122888 | tf_op jit(solution)/shard_map/ppermute | solution.py:161
  14.9 1.8 %collective-permute-done = bf16[2,80,128]{2,1,0:T(8,128)(2,1)S(1)} collective-permute-done((bf16[2,80,128]{2,1,0:T(8,128)(2,1)S(1)}, bf16[2,80,128]{2,1,0:T(8,128)(2,1)S(1)}, u32[]{:S(2)}, u32[]{:S(2)}) %collective-permute-start) | collective-permute-done | bytes 40992 | tf_op jit(solution)/shard_map/ppermute | solution.py:161
  16.9 0.2 broadcast_in_dim.12
  17.0 0.5 pad_maximum_fusion
  17.5 0.0 collective-permute-done.1
  17.5 25.8 %all_to_all.10 = bf16[64,10,2,128]{3,2,1,0:T(2,128)(2,1)S(1)} all-to-all(bf16[64,10,2,128]{3,2,1,0:T(2,128)(2,1)S(1)} %pad_maximum_fusion), channel_id=1, replica_groups=mesh['layer'=4,'train'=8,'query'=8] {'query','train'}, dimensions={0} | all-to-all | bytes 655360 | tf_op jit(solution)/shard_map/all_to_all | solution.py:171
  43.3 0.2 slice.48
  43.5 0.2 convolution_bitcast_fusion.1
  43.7 0.2 convolution_bitcast_fusion
  44.1 0.2 convolution_bitcast_fusion.2
  44.3 0.1 reshape.65
  44.4 0.1 copy.25
  44.5 0.1 broadcast_in_dim.13
  44.7 21.9 %all_to_all.11 = f32[256,1,64]{2,1,0:T(1,128)S(1)} all-to-all(f32[256,1,64]{2,1,0:T(1,128)S(1)} %bitcast.62), channel_id=1, replica_groups=mesh['layer'=4,'train'=8,'query'=8] {'layer','train','query'}, dimensions={0} | all-to-all | bytes 131072 | tf_op jit(solution)/shard_map/all_to_all | solution.py:194
  66.6 0.7 %add_shares.1 = f32[8,8]{1,0:T(8,128)} custom-call(f32[256,64]{1,0:T(8,128)S(1)} %bitcast.53), custom_call_target="tpu_custom_call" | custom-call | tf_op jit(solution)/shard_map/add_shares/pallas_call | solution.py:195
  (17 shorter events, 0.3 us)
Async XLA Ops:
  1.3 16.2 %collective-permute-start.1 = (bf16[2,8,128,128]{3,2,0,1:T(8,128)(2,1)S(1)}, bf16[2,8,128,128]{3,2,0,1:T(8,128)(2,1)S(1)}, u32[]{:S(2)}, u32[]{:S(2)}) collective-permute-start(bf16[2,8,128,128]{3,2,0,1:T(8,128)(2,1)S(1)} %bitcast.63), channel_id=1, source_target_pairs={{0,8},{8,0},{16,24},{24,16},{32,40},{40,32},{48,56},{56,48},{1,9},... | collective-permute-start | bytes 1572872 | tf_op jit(solution)/shard_map/ppermute | solution.py:150
  13.8 2.9 %collective-permute-start = (bf16[2,80,128]{2,1,0:T(8,128)(2,1)S(1)}, bf16[2,80,128]{2,1,0:T(8,128)(2,1)S(1)}, u32[]{:S(2)}, u32[]{:S(2)}) collective-permute-start(bf16[2,80,128]{2,1,0:T(8,128)(2,1)S(1)} %pad_maximum_fusion.1), channel_id=1, source_target_pairs={{0,128},{64,192},{128,0},{192,64},{1,129},{65,193},{129,1},{193,65... | collective-permute-start | bytes 122888 | tf_op jit(solution)/shard_map/ppermute | solution.py:161

commit v4 on v3

--- a/solution.py
+++ b/solution.py
@@ -21,8 +21,6 @@
     result,
     act,
     grad,
-    in_weights,
-    out_weights,
     inner,
     outer,
     arrived,
@@ -34,10 +32,8 @@
     for step in range(CHUNKS):
         cols = pl.ds(step * chunk, chunk)
         group = [
-            (in_projection.at[cols], in_weights.at[cols]),
             (train_act.at[:, :, cols], act.at[pl.ds(0, ckpts), :, cols]),
             (query_act.at[:, :, cols], act.at[pl.ds(ckpts, ckpts), :, cols]),
-            (out_projection.at[:, cols], out_weights.at[:, cols]),
             (train_grad.at[:, :, cols], grad.at[pl.ds(0, ckpts), :, cols]),
             (query_grad.at[:, :, cols], grad.at[pl.ds(ckpts, ckpts), :, cols]),
         ]
@@ -58,12 +54,12 @@
                 copy.start()
         inner_term = jnp.dot(
             act[:, :, cols].reshape(rows, chunk),
-            in_weights[cols],
+            in_projection[cols],
             preferred_element_type=jnp.float32,
         )
         outer_term = lax.dot_general(
             grad[:, :, cols].reshape(rows, chunk),
-            out_weights[:, cols],
+            out_projection[:, cols],
             (((1,), (1,)), ((), ())),
             preferred_element_type=jnp.float32,
         )
@@ -94,22 +90,21 @@
     flat = [x.reshape(ckpts, seq_len, width) for x in (train_act, train_grad, query_act, query_grad)]
     stay = pl.BlockSpec(memory_space=pl.ANY)
     scalar = pl.BlockSpec(memory_space=pltpu.SMEM)
+    held = pl.BlockSpec(memory_space=pltpu.VMEM)
     rows = 2 * ckpts * seq_len
     return pl.pallas_call(
         sketch_kernel,
         out_shape=jax.ShapeDtypeStruct((2, ckpts, outs, ins), jnp.float32),
-        in_specs=[scalar, scalar] + [stay] * 6,
+        in_specs=[scalar, scalar] + [stay] * 4 + [held] * 2,
         out_specs=pl.BlockSpec(memory_space=pltpu.VMEM),
         scratch_shapes=[
             pltpu.VMEM((2 * ckpts, seq_len, width), jnp.bfloat16),
             pltpu.VMEM((2 * ckpts, seq_len, width), jnp.bfloat16),
-            pltpu.VMEM((width, ins), jnp.bfloat16),
-            pltpu.VMEM((outs, width), jnp.bfloat16),
             pltpu.VMEM((rows, ins), jnp.float32),
             pltpu.VMEM((rows, outs), jnp.float32),
-            pltpu.SemaphoreType.DMA((CHUNKS, 6)),
+            pltpu.SemaphoreType.DMA((CHUNKS, 4)),
         ],
-        compiler_params=pltpu.CompilerParams(vmem_limit_bytes=60 * 1024 * 1024),
+        compiler_params=pltpu.CompilerParams(vmem_limit_bytes=52 * 1024 * 1024),
         name="sketches",
     )(train_length, query_length, *flat, in_projection[0], out_projection[0].T)
 

time: 67.5 us -> 66.5 us (0.985)
  Pallas kernels: 6.54 us -> 5.39 us
    pallas_call x1, Pallas kernels: 5.83 us -> 4.68 us  [sketches(): pl.pallas_call(sketch_kernel, out_shape=jax.ShapeDtypeStruct((2, ckpts, o...]
  transfers between devices with their start and end apart: 2 -> 2, of which waited for: 1 -> 1; matrix products, arithmetic and copies ran while one was open for 1% -> 1% of each run, Pallas kernels for 9% -> 7%
where the time goes in v4:
time: 66.5 us; the launch traced here: 66.3 us
  blocking collectives  50.5 us (76%)
  Pallas kernels  5.39 us (8%)
  starting transfers between devices  3.26 us (5%)
  local copies, waits for them, and re-layouts  2.38 us (4%)
  waiting for transfers between devices  2.1 us (3%)
  between operations  1.53 us (2%)
    all_to_all x1, blocking collectives, on_device(): received = lax.all_to_all(message, ('query', 'train'), 0, 0)  25.7 us
    all_to_all x1, blocking collectives, on_device(): shares = lax.all_to_all(tiles, ('layer', 'train', 'query'), 0, 0)  21.9 us
    pallas_call x1, Pallas kernels, sketches(): pl.pallas_call(sketch_kernel, out_shape=jax.ShapeDtypeStruct((2, ckpts, o...  4.68 us
    all_gather x1, blocking collectives, on_device(): lax.all_gather(terms, 'layer', axis_index_groups=[[i, i + 1] for i in ran...  2.84 us
    ppermute x1, starting transfers between devices, on_device(): hessian_other = lax.ppermute(other_half, 'train', swap)  2.13 us
    ppermute x1, waiting for transfers between devices, on_device(): lax.ppermute(outgoing, 'layer', [(i, i ^ 2) for i in range(layers)])  2.1 us
    dynamic_slice x1, local copies, waits for them, and re-layouts, on_device(): hessian_own = lax.dynamic_index_in_dim(hessian, parity, 1, keepdims=False)  1.39 us
  transfers between devices with their start and end apart: 2, of which 1 were waited for; matrix products, arithmetic and copies ran while one was open for 1% of the time, Pallas kernels for 7%

profile of v4, /device:TPU:1, one launch (start us, length us, event | category | flops | bytes accessed | tf_op | source)
XLA Modules:
  0.0 66.3 jit_solution(11758184253997406234)
XLA Ops:
  0.0 0.0 copy-start
  0.0 0.0 copy-start.1
  0.0 1.4 %constant_dynamic-slice_fusion = (bf16[2,1,8,128,128]{4,3,2,1,0:T(8,128)(2,1)S(1)}, bf16[2,1,8,128,128]{4,3,2,1,0:T(8,128)(2,1)S(1)}) fusion(bf16[2,2,8,128,128]{4,3,2,1,0:T(8,128)(2,1)} %bitcast.62, s32[]{:T(128)S(6)} %select_n.16, s32[]{:T(128)S(6)} %select_n.15), kind=kLoop, calls=%fused_computation.28 | loop fusion | bytes 2097160 | tf_op jit(solution)/shard_map/jit(dynamic_index_in_dim)/dynamic_slice | solution.py:146
  1.4 2.1 %collective-permute-start.1 = (bf16[2,8,128,128]{3,2,0,1:T(8,128)(2,1)S(1)}, bf16[2,8,128,128]{3,2,0,1:T(8,128)(2,1)S(1)}, u32[]{:S(2)}, u32[]{:S(2)}) collective-permute-start(bf16[2,8,128,128]{3,2,0,1:T(8,128)(2,1)S(1)} %bitcast.64), channel_id=1, source_target_pairs={{0,8},{8,0},{16,24},{24,16},{32,40},{40,32},{48,56},{56,48},{1,9},... | collective-permute-start | bytes 1572872 | tf_op jit(solution)/shard_map/ppermute | solution.py:145
  4.9 0.0 copy-done
  4.9 0.0 copy-done.1
  4.9 4.7 %sketches.1 = f32[2,2,64,128]{3,2,1,0:T(8,128)S(1)} custom-call(s32[1]{0:T(128)S(6)} %copy.40.train_length, s32[1]{0:T(128)S(6)} %copy.41.query_length, bf16[2,128,4096]{2,1,0:T(8,128)(2,1)} %bitcast.56, bf16[2,128,4096]{2,1,0:T(8,128)(2,1)} %bitcast.57, bf16[2,128,4096]{2,1,0:T(8,128)(2,1)} %bitcast.58, bf16[2,128,4096]{2,1,0:T(8,128)(2,1)} %bitcast.59, ...), custom_call_target="tpu_custom_call" | custom-call | tf_op jit(solution)/shard_map/sketches/pallas_call | solution.py:95
  9.6 2.8 %all-gather = f32[4,2,64,128]{3,2,1,0:T(8,128)S(1)} all-gather(f32[2,2,64,128]{3,2,1,0:T(8,128)S(1)} %sketches.1), channel_id=2, replica_groups={{0,64},{128,192},{1,65},{129,193},{2,66},{130,194},{3,67},{131,195},{4,..., dimensions={0}, use_global_device_ids=true | all-gather | bytes 393216 | tf_op jit(solution)/shard_map/all_gather | solution.py:148
  12.5 1.1 %collective-permute-start = (bf16[2,80,128]{2,1,0:T(8,128)(2,1)S(1)}, bf16[2,80,128]{2,1,0:T(8,128)(2,1)S(1)}, u32[]{:S(2)}, u32[]{:S(2)}) collective-permute-start(bf16[2,80,128]{2,1,0:T(8,128)(2,1)S(1)} %pad_maximum_fusion.1), channel_id=1, source_target_pairs={{0,128},{64,192},{128,0},{192,64},{1,129},{65,193},{129,1},{193,65... | collective-permute-start | bytes 122888 | tf_op jit(solution)/shard_map/ppermute | solution.py:156
  13.7 2.1 %collective-permute-done = bf16[2,80,128]{2,1,0:T(8,128)(2,1)S(1)} collective-permute-done((bf16[2,80,128]{2,1,0:T(8,128)(2,1)S(1)}, bf16[2,80,128]{2,1,0:T(8,128)(2,1)S(1)}, u32[]{:S(2)}, u32[]{:S(2)}) %collective-permute-start) | collective-permute-done | bytes 40992 | tf_op jit(solution)/shard_map/ppermute | solution.py:156
  15.9 0.2 broadcast_in_dim.12
  16.1 0.5 pad_maximum_fusion
  16.6 0.0 collective-permute-done.1
  16.6 25.7 %all_to_all.10 = bf16[64,10,2,128]{3,2,1,0:T(2,128)(2,1)S(1)} all-to-all(bf16[64,10,2,128]{3,2,1,0:T(2,128)(2,1)S(1)} %pad_maximum_fusion), channel_id=1, replica_groups=mesh['layer'=4,'train'=8,'query'=8] {'query','train'}, dimensions={0} | all-to-all | bytes 655360 | tf_op jit(solution)/shard_map/all_to_all | solution.py:166
  42.3 0.2 slice.48
  42.5 0.2 convolution_bitcast_fusion.1
  42.7 0.2 convolution_bitcast_fusion
  43.1 0.2 convolution_bitcast_fusion.2
  43.3 0.1 reshape.65
  43.4 0.1 copy.25
  43.5 0.1 broadcast_in_dim.13
  43.7 21.9 %all_to_all.11 = f32[256,1,64]{2,1,0:T(1,128)S(1)} all-to-all(f32[256,1,64]{2,1,0:T(1,128)S(1)} %bitcast.63), channel_id=1, replica_groups=mesh['layer'=4,'train'=8,'query'=8] {'layer','train','query'}, dimensions={0} | all-to-all | bytes 131072 | tf_op jit(solution)/shard_map/all_to_all | solution.py:189
  65.6 0.7 %add_shares.1 = f32[8,8]{1,0:T(8,128)} custom-call(f32[256,64]{1,0:T(8,128)S(1)} %bitcast.54), custom_call_target="tpu_custom_call" | custom-call | tf_op jit(solution)/shard_map/add_shares/pallas_call | solution.py:190
  (17 shorter events, 0.3 us)
Async XLA Ops:
  0.0 4.9 %copy-start = (bf16[1,4096,128]{2,1,0:T(8,128)(2,1)S(1)}, bf16[1,4096,128]{2,1,0:T(8,128)(2,1)}, u32[]{:S(2)}) copy-start(bf16[1,4096,128]{2,1,0:T(8,128)(2,1)} %param.13) | copy-start | bytes 3145732
  0.0 4.9 %copy-start.1 = (bf16[1,4096,64]{1,2,0:T(8,128)(2,1)S(1)}, bf16[1,4096,64]{1,2,0:T(8,128)(2,1)}, u32[]{:S(2)}) copy-start(bf16[1,4096,64]{1,2,0:T(8,128)(2,1)} %param.14) | copy-start | bytes 1572868
  1.4 15.1 %collective-permute-start.1 = (bf16[2,8,128,128]{3,2,0,1:T(8,128)(2,1)S(1)}, bf16[2,8,128,128]{3,2,0,1:T(8,128)(2,1)S(1)}, u32[]{:S(2)}, u32[]{:S(2)}) collective-permute-start(bf16[2,8,128,128]{3,2,0,1:T(8,128)(2,1)S(1)} %bitcast.64), channel_id=1, source_target_pairs={{0,8},{8,0},{16,24},{24,16},{32,40},{40,32},{48,56},{56,48},{1,9},... | collective-permute-start | bytes 1572872 | tf_op jit(solution)/shard_map/ppermute | solution.py:145
  12.5 3.2 %collective-permute-start = (bf16[2,80,128]{2,1,0:T(8,128)(2,1)S(1)}, bf16[2,80,128]{2,1,0:T(8,128)(2,1)S(1)}, u32[]{:S(2)}, u32[]{:S(2)}) collective-permute-start(bf16[2,80,128]{2,1,0:T(8,128)(2,1)S(1)} %pad_maximum_fusion.1), channel_id=1, source_target_pairs={{0,128},{64,192},{128,0},{192,64},{1,129},{65,193},{129,1},{193,65... | collective-permute-start | bytes 122888 | tf_op jit(solution)/shard_map/ppermute | solution.py:156

commit v5 on v4

--- a/solution.py
+++ b/solution.py
@@ -6,7 +6,7 @@
 from jax.sharding import PartitionSpec as P
 
 CHUNKS = 4
-AHEAD = 3
+AHEAD = 4
 
 
 def sketch_kernel(
@@ -156,12 +156,13 @@
     incoming = lax.ppermute(outgoing, "layer", [(i, i ^ 2) for i in range(layers)])
     features = ((own + incoming.astype(jnp.float32)) / seq_len).astype(jnp.bfloat16)
     train_block = jnp.transpose(features[:, :block].reshape(ckpts, 2, half, ins), (1, 2, 0, 3))
-    train_message = jnp.broadcast_to(train_block, (cols_b, pairs, 2, half, ckpts, ins))
-    train_message = train_message.reshape(grid, half, ckpts, ins)
     query = features[:, block:].reshape(ckpts, pairs, 2, cols_b, ins)
-    query_own = jnp.transpose(query, (3, 1, 2, 0, 4)).reshape(grid, 1, ckpts, ins)
-    query_other = jnp.transpose(jnp.flip(query, 2), (3, 1, 2, 0, 4)).reshape(grid, 1, ckpts, ins)
-    message = jnp.concatenate([train_message, query_own, query_other], axis=1)
+    query_own = jnp.transpose(query, (3, 1, 2, 0, 4))[:, :, :, None]
+    query_other = jnp.transpose(jnp.stack([query[:, :, 1], query[:, :, 0]], axis=2), (3, 1, 2, 0, 4))[:, :, :, None]
+    row = lax.broadcasted_iota(jnp.int32, (cols_b, pairs, 2, half + 2, ckpts, ins), 3)
+    train_rows = jnp.pad(train_block, ((0, 0), (0, 2), (0, 0), (0, 0)))
+    message = jnp.where(row < half, train_rows, jnp.where(row == half, query_own, query_other))
+    message = message.reshape(grid, half + 2, ckpts, ins)
     message, hessian_other = lax.optimization_barrier((message, hessian_other))
     received = lax.all_to_all(message, ("query", "train"), 0, 0)
     train_rows = received[:, :half]

time: 66.5 us -> 66.4 us (level)
  no operation moved by 1% of the time
where the time goes in v5:
time: 66.4 us; the launch traced here: 66.2 us
  blocking collectives  50.5 us (76%)
  Pallas kernels  5.34 us (8%)
  starting transfers between devices  3.26 us (5%)
  local copies, waits for them, and re-layouts  2.3 us (3%)
  waiting for transfers between devices  2.1 us (3%)
  between operations  1.55 us (2%)
    all_to_all x1, blocking collectives, on_device(): received = lax.all_to_all(message, ('query', 'train'), 0, 0)  25.7 us
    all_to_all x1, blocking collectives, on_device(): shares = lax.all_to_all(tiles, ('layer', 'train', 'query'), 0, 0)  21.9 us
    pallas_call x1, Pallas kernels, sketches(): pl.pallas_call(sketch_kernel, out_shape=jax.ShapeDtypeStruct((2, ckpts, o...  4.64 us
    all_gather x1, blocking collectives, on_device(): lax.all_gather(terms, 'layer', axis_index_groups=[[i, i + 1] for i in ran...  2.84 us
    ppermute x1, starting transfers between devices, on_device(): hessian_other = lax.ppermute(other_half, 'train', swap)  2.13 us
    ppermute x1, waiting for transfers between devices, on_device(): lax.ppermute(outgoing, 'layer', [(i, i ^ 2) for i in range(layers)])  2.1 us
    dynamic_slice x1, local copies, waits for them, and re-layouts, on_device(): hessian_own = lax.dynamic_index_in_dim(hessian, parity, 1, keepdims=False)  1.39 us
  transfers between devices with their start and end apart: 2, of which 1 were waited for; matrix products, arithmetic and copies ran while one was open for 1% of the time, Pallas kernels for 7%

profile of v5, /device:TPU:1, one launch (start us, length us, event | category | flops | bytes accessed | tf_op | source)
XLA Modules:
  0.0 66.2 jit_solution(12005570370812192675)
XLA Ops:
  0.0 0.0 copy-start
  0.0 0.0 copy-start.1
  0.0 1.4 %constant_dynamic-slice_fusion = (bf16[2,1,8,128,128]{4,3,2,1,0:T(8,128)(2,1)S(1)}, bf16[2,1,8,128,128]{4,3,2,1,0:T(8,128)(2,1)S(1)}) fusion(bf16[2,2,8,128,128]{4,3,2,1,0:T(8,128)(2,1)} %bitcast.64, s32[]{:T(128)S(6)} %select_n.28, s32[]{:T(128)S(6)} %select_n.27), kind=kLoop, calls=%fused_computation.29 | loop fusion | bytes 2097160 | tf_op jit(solution)/shard_map/jit(dynamic_index_in_dim)/dynamic_slice | solution.py:146
  1.4 2.1 %collective-permute-start.1 = (bf16[2,8,128,128]{3,2,0,1:T(8,128)(2,1)S(1)}, bf16[2,8,128,128]{3,2,0,1:T(8,128)(2,1)S(1)}, u32[]{:S(2)}, u32[]{:S(2)}) collective-permute-start(bf16[2,8,128,128]{3,2,0,1:T(8,128)(2,1)S(1)} %bitcast.66), channel_id=1, source_target_pairs={{0,8},{8,0},{16,24},{24,16},{32,40},{40,32},{48,56},{56,48},{1,9},... | collective-permute-start | bytes 1572872 | tf_op jit(solution)/shard_map/ppermute | solution.py:145
  4.9 0.0 copy-done
  4.9 0.0 copy-done.1
  4.9 4.6 %sketches.1 = f32[2,2,64,128]{3,2,1,0:T(8,128)S(1)} custom-call(s32[1]{0:T(128)S(6)} %copy.45.train_length, s32[1]{0:T(128)S(6)} %copy.46.query_length, bf16[2,128,4096]{2,1,0:T(8,128)(2,1)} %bitcast.59, bf16[2,128,4096]{2,1,0:T(8,128)(2,1)} %bitcast.60, bf16[2,128,4096]{2,1,0:T(8,128)(2,1)} %bitcast.61, bf16[2,128,4096]{2,1,0:T(8,128)(2,1)} %bitcast.62, ...), custom_call_target="tpu_custom_call" | custom-call | tf_op jit(solution)/shard_map/sketches/pallas_call | solution.py:95
  9.5 2.8 %all-gather = f32[4,2,64,128]{3,2,1,0:T(8,128)S(1)} all-gather(f32[2,2,64,128]{3,2,1,0:T(8,128)S(1)} %sketches.1), channel_id=2, replica_groups={{0,64},{128,192},{1,65},{129,193},{2,66},{130,194},{3,67},{131,195},{4,..., dimensions={0}, use_global_device_ids=true | all-gather | bytes 393216 | tf_op jit(solution)/shard_map/all_gather | solution.py:148
  12.5 1.1 %collective-permute-start = (bf16[2,80,128]{2,1,0:T(8,128)(2,1)S(1)}, bf16[2,80,128]{2,1,0:T(8,128)(2,1)S(1)}, u32[]{:S(2)}, u32[]{:S(2)}) collective-permute-start(bf16[2,80,128]{2,1,0:T(8,128)(2,1)S(1)} %pad_maximum_fusion), channel_id=1, source_target_pairs={{0,128},{64,192},{128,0},{192,64},{1,129},{65,193},{129,1},{193,65... | collective-permute-start | bytes 122888 | tf_op jit(solution)/shard_map/ppermute | solution.py:156
  13.6 2.1 %collective-permute-done = bf16[2,80,128]{2,1,0:T(8,128)(2,1)S(1)} collective-permute-done((bf16[2,80,128]{2,1,0:T(8,128)(2,1)S(1)}, bf16[2,80,128]{2,1,0:T(8,128)(2,1)S(1)}, u32[]{:S(2)}, u32[]{:S(2)}) %collective-permute-start) | collective-permute-done | bytes 40992 | tf_op jit(solution)/shard_map/ppermute | solution.py:156
  15.8 0.1 pad_maximum_fusion.1
  16.1 0.3 broadcast_select_fusion
  16.4 0.0 collective-permute-done.1
  16.4 25.7 %all_to_all.10 = bf16[64,10,2,128]{3,2,1,0:T(2,128)(2,1)S(1)} all-to-all(bf16[64,10,2,128]{3,2,1,0:T(2,128)(2,1)S(1)} %broadcast_select_fusion), channel_id=1, replica_groups=mesh['layer'=4,'train'=8,'query'=8] {'query','train'}, dimensions={0} | all-to-all | bytes 655360 | tf_op jit(solution)/shard_map/all_to_all | solution.py:167
  42.2 0.2 slice.58
  42.3 0.2 convolution_bitcast_fusion.1
  42.6 0.2 convolution_bitcast_fusion
  42.9 0.2 convolution_bitcast_fusion.2
  43.1 0.1 reshape.61
  43.2 0.1 copy.27
  43.4 0.1 broadcast_in_dim.43
  43.5 21.9 %all_to_all.11 = f32[256,1,64]{2,1,0:T(1,128)S(1)} all-to-all(f32[256,1,64]{2,1,0:T(1,128)S(1)} %bitcast.65), channel_id=1, replica_groups=mesh['layer'=4,'train'=8,'query'=8] {'layer','train','query'}, dimensions={0} | all-to-all | bytes 131072 | tf_op jit(solution)/shard_map/all_to_all | solution.py:190
  65.5 0.7 %add_shares.1 = f32[8,8]{1,0:T(8,128)} custom-call(f32[256,64]{1,0:T(8,128)S(1)} %bitcast.57), custom_call_target="tpu_custom_call" | custom-call | tf_op jit(solution)/shard_map/add_shares/pallas_call | solution.py:191
  (21 shorter events, 0.4 us)
Async XLA Ops:
  0.0 4.9 %copy-start = (bf16[1,4096,128]{2,1,0:T(8,128)(2,1)S(1)}, bf16[1,4096,128]{2,1,0:T(8,128)(2,1)}, u32[]{:S(2)}) copy-start(bf16[1,4096,128]{2,1,0:T(8,128)(2,1)} %param.13) | copy-start | bytes 3145732
  0.0 4.9 %copy-start.1 = (bf16[1,4096,64]{1,2,0:T(8,128)(2,1)S(1)}, bf16[1,4096,64]{1,2,0:T(8,128)(2,1)}, u32[]{:S(2)}) copy-start(bf16[1,4096,64]{1,2,0:T(8,128)(2,1)} %param.14) | copy-start | bytes 1572868
  1.4 15.0 %collective-permute-start.1 = (bf16[2,8,128,128]{3,2,0,1:T(8,128)(2,1)S(1)}, bf16[2,8,128,128]{3,2,0,1:T(8,128)(2,1)S(1)}, u32[]{:S(2)}, u32[]{:S(2)}) collective-permute-start(bf16[2,8,128,128]{3,2,0,1:T(8,128)(2,1)S(1)} %bitcast.66), channel_id=1, source_target_pairs={{0,8},{8,0},{16,24},{24,16},{32,40},{40,32},{48,56},{56,48},{1,9},... | collective-permute-start | bytes 1572872 | tf_op jit(solution)/shard_map/ppermute | solution.py:145
  12.5 3.2 %collective-permute-start = (bf16[2,80,128]{2,1,0:T(8,128)(2,1)S(1)}, bf16[2,80,128]{2,1,0:T(8,128)(2,1)S(1)}, u32[]{:S(2)}, u32[]{:S(2)}) collective-permute-start(bf16[2,80,128]{2,1,0:T(8,128)(2,1)S(1)} %pad_maximum_fusion), channel_id=1, source_target_pairs={{0,128},{64,192},{128,0},{192,64},{1,129},{65,193},{129,1},{193,65... | collective-permute-start | bytes 122888 | tf_op jit(solution)/shard_map/ppermute | solution.py:156

commit v6 on v5

--- a/solution.py
+++ b/solution.py
@@ -184,10 +184,10 @@
     tile_rows = scores.shape[0] // rows_a
     tile_cols = scores.shape[1] // cols_b
     tiles = scores.reshape(cols_b, rows_a, tile_cols, cols_b)
-    tiles = jnp.transpose(tiles, (1, 3, 0, 2)).reshape(1, grid, 1, tile_rows * tile_cols)
-    tiles = jnp.broadcast_to(tiles, (layers, grid, 1, tile_rows * tile_cols))
+    tiles = jnp.transpose(tiles, (3, 1, 0, 2)).reshape(grid, 1, 1, tile_rows * tile_cols)
+    tiles = jnp.broadcast_to(tiles, (grid, layers, 1, tile_rows * tile_cols))
     tiles = tiles.reshape(layers * grid, 1, tile_rows * tile_cols)
-    shares = lax.all_to_all(tiles, ("layer", "train", "query"), 0, 0)
+    shares = lax.all_to_all(tiles, ("query", "train", "layer"), 0, 0)
     return pl.pallas_call(
         add_shares,
         out_shape=jax.ShapeDtypeStruct((tile_rows, tile_cols), jnp.float32),

time: 66.4 us -> 66.5 us (level)
  no operation moved by 1% of the time
where the time goes in v6:
time: 66.5 us; the launch traced here: 66.3 us
  blocking collectives  50.5 us (76%)
  Pallas kernels  5.34 us (8%)
  starting transfers between devices  3.26 us (5%)
  local copies, waits for them, and re-layouts  2.42 us (4%)
  waiting for transfers between devices  2.1 us (3%)
  between operations  1.55 us (2%)
    all_to_all x1, blocking collectives, on_device(): received = lax.all_to_all(message, ('query', 'train'), 0, 0)  25.7 us
    all_to_all x1, blocking collectives, on_device(): shares = lax.all_to_all(tiles, ('query', 'train', 'layer'), 0, 0)  21.9 us
    pallas_call x1, Pallas kernels, sketches(): pl.pallas_call(sketch_kernel, out_shape=jax.ShapeDtypeStruct((2, ckpts, o...  4.64 us
    all_gather x1, blocking collectives, on_device(): lax.all_gather(terms, 'layer', axis_index_groups=[[i, i + 1] for i in ran...  2.84 us
    ppermute x1, starting transfers between devices, on_device(): hessian_other = lax.ppermute(other_half, 'train', swap)  2.13 us
    ppermute x1, waiting for transfers between devices, on_device(): lax.ppermute(outgoing, 'layer', [(i, i ^ 2) for i in range(layers)])  2.1 us
    dynamic_slice x1, local copies, waits for them, and re-layouts, on_device(): hessian_own = lax.dynamic_index_in_dim(hessian, parity, 1, keepdims=False)  1.39 us
  transfers between devices with their start and end apart: 2, of which 1 were waited for; matrix products, arithmetic and copies ran while one was open for 1% of the time, Pallas kernels for 7%

profile of v6, /device:TPU:1, one launch (start us, length us, event | category | flops | bytes accessed | tf_op | source)
XLA Modules:
  0.0 66.3 jit_solution(7957488549544292888)
XLA Ops:
  0.0 0.0 copy-start
  0.0 0.0 copy-start.1
  0.0 1.4 %constant_dynamic-slice_fusion = (bf16[2,1,8,128,128]{4,3,2,1,0:T(8,128)(2,1)S(1)}, bf16[2,1,8,128,128]{4,3,2,1,0:T(8,128)(2,1)S(1)}) fusion(bf16[2,2,8,128,128]{4,3,2,1,0:T(8,128)(2,1)} %bitcast.64, s32[]{:T(128)S(6)} %select_n.28, s32[]{:T(128)S(6)} %select_n.27), kind=kLoop, calls=%fused_computation.29 | loop fusion | bytes 2097160 | tf_op jit(solution)/shard_map/jit(dynamic_index_in_dim)/dynamic_slice | solution.py:146
  1.4 2.1 %collective-permute-start.1 = (bf16[2,8,128,128]{3,2,0,1:T(8,128)(2,1)S(1)}, bf16[2,8,128,128]{3,2,0,1:T(8,128)(2,1)S(1)}, u32[]{:S(2)}, u32[]{:S(2)}) collective-permute-start(bf16[2,8,128,128]{3,2,0,1:T(8,128)(2,1)S(1)} %bitcast.66), channel_id=1, source_target_pairs={{0,8},{8,0},{16,24},{24,16},{32,40},{40,32},{48,56},{56,48},{1,9},... | collective-permute-start | bytes 1572872 | tf_op jit(solution)/shard_map/ppermute | solution.py:145
  4.9 0.0 copy-done
  4.9 0.0 copy-done.1
  4.9 4.6 %sketches.1 = f32[2,2,64,128]{3,2,1,0:T(8,128)S(1)} custom-call(s32[1]{0:T(128)S(6)} %copy.45.train_length, s32[1]{0:T(128)S(6)} %copy.46.query_length, bf16[2,128,4096]{2,1,0:T(8,128)(2,1)} %bitcast.59, bf16[2,128,4096]{2,1,0:T(8,128)(2,1)} %bitcast.60, bf16[2,128,4096]{2,1,0:T(8,128)(2,1)} %bitcast.61, bf16[2,128,4096]{2,1,0:T(8,128)(2,1)} %bitcast.62, ...), custom_call_target="tpu_custom_call" | custom-call | tf_op jit(solution)/shard_map/sketches/pallas_call | solution.py:95
  9.5 2.8 %all-gather = f32[4,2,64,128]{3,2,1,0:T(8,128)S(1)} all-gather(f32[2,2,64,128]{3,2,1,0:T(8,128)S(1)} %sketches.1), channel_id=2, replica_groups={{0,64},{128,192},{1,65},{129,193},{2,66},{130,194},{3,67},{131,195},{4,..., dimensions={0}, use_global_device_ids=true | all-gather | bytes 393216 | tf_op jit(solution)/shard_map/all_gather | solution.py:148
  12.5 1.1 %collective-permute-start = (bf16[2,80,128]{2,1,0:T(8,128)(2,1)S(1)}, bf16[2,80,128]{2,1,0:T(8,128)(2,1)S(1)}, u32[]{:S(2)}, u32[]{:S(2)}) collective-permute-start(bf16[2,80,128]{2,1,0:T(8,128)(2,1)S(1)} %pad_maximum_fusion), channel_id=1, source_target_pairs={{0,128},{64,192},{128,0},{192,64},{1,129},{65,193},{129,1},{193,65... | collective-permute-start | bytes 122888 | tf_op jit(solution)/shard_map/ppermute | solution.py:156
  13.6 2.1 %collective-permute-done = bf16[2,80,128]{2,1,0:T(8,128)(2,1)S(1)} collective-permute-done((bf16[2,80,128]{2,1,0:T(8,128)(2,1)S(1)}, bf16[2,80,128]{2,1,0:T(8,128)(2,1)S(1)}, u32[]{:S(2)}, u32[]{:S(2)}) %collective-permute-start) | collective-permute-done | bytes 40992 | tf_op jit(solution)/shard_map/ppermute | solution.py:156
  15.8 0.1 pad_maximum_fusion.1
  16.1 0.3 broadcast_select_fusion
  16.4 0.0 collective-permute-done.1
  16.4 25.7 %all_to_all.10 = bf16[64,10,2,128]{3,2,1,0:T(2,128)(2,1)S(1)} all-to-all(bf16[64,10,2,128]{3,2,1,0:T(2,128)(2,1)S(1)} %broadcast_select_fusion), channel_id=1, replica_groups=mesh['layer'=4,'train'=8,'query'=8] {'query','train'}, dimensions={0} | all-to-all | bytes 655360 | tf_op jit(solution)/shard_map/all_to_all | solution.py:167
  42.2 0.2 slice.58
  42.3 0.2 convolution_bitcast_fusion.1
  42.6 0.2 convolution_bitcast_fusion
  42.9 0.2 convolution_bitcast_fusion.2
  43.1 0.1 reshape.61
  43.2 0.3 copy.27
  43.5 0.1 broadcast_in_dim.43
  43.7 21.9 %all_to_all.11 = f32[256,1,64]{2,1,0:T(1,128)S(1)} all-to-all(f32[256,1,64]{2,1,0:T(1,128)S(1)} %bitcast.65), channel_id=1, replica_groups=mesh['layer'=4,'train'=8,'query'=8] {'query','train','layer'}, dimensions={0} | all-to-all | bytes 131072 | tf_op jit(solution)/shard_map/all_to_all | solution.py:190
  65.6 0.7 %add_shares.1 = f32[8,8]{1,0:T(8,128)} custom-call(f32[256,64]{1,0:T(8,128)S(1)} %bitcast.57), custom_call_target="tpu_custom_call" | custom-call | tf_op jit(solution)/shard_map/add_shares/pallas_call | solution.py:191
  (21 shorter events, 0.4 us)
Async XLA Ops:
  0.0 4.9 %copy-start = (bf16[1,4096,128]{2,1,0:T(8,128)(2,1)S(1)}, bf16[1,4096,128]{2,1,0:T(8,128)(2,1)}, u32[]{:S(2)}) copy-start(bf16[1,4096,128]{2,1,0:T(8,128)(2,1)} %param.13) | copy-start | bytes 3145732
  0.0 4.9 %copy-start.1 = (bf16[1,4096,64]{1,2,0:T(8,128)(2,1)S(1)}, bf16[1,4096,64]{1,2,0:T(8,128)(2,1)}, u32[]{:S(2)}) copy-start(bf16[1,4096,64]{1,2,0:T(8,128)(2,1)} %param.14) | copy-start | bytes 1572868
  1.4 15.0 %collective-permute-start.1 = (bf16[2,8,128,128]{3,2,0,1:T(8,128)(2,1)S(1)}, bf16[2,8,128,128]{3,2,0,1:T(8,128)(2,1)S(1)}, u32[]{:S(2)}, u32[]{:S(2)}) collective-permute-start(bf16[2,8,128,128]{3,2,0,1:T(8,128)(2,1)S(1)} %bitcast.66), channel_id=1, source_target_pairs={{0,8},{8,0},{16,24},{24,16},{32,40},{40,32},{48,56},{56,48},{1,9},... | collective-permute-start | bytes 1572872 | tf_op jit(solution)/shard_map/ppermute | solution.py:145
  12.5 3.2 %collective-permute-start = (bf16[2,80,128]{2,1,0:T(8,128)(2,1)S(1)}, bf16[2,80,128]{2,1,0:T(8,128)(2,1)S(1)}, u32[]{:S(2)}, u32[]{:S(2)}) collective-permute-start(bf16[2,80,128]{2,1,0:T(8,128)(2,1)S(1)} %pad_maximum_fusion), channel_id=1, source_target_pairs={{0,128},{64,192},{128,0},{192,64},{1,129},{65,193},{129,1},{193,65... | collective-permute-start | bytes 122888 | tf_op jit(solution)/shard_map/ppermute | solution.py:156
